TPU v7x, 512 devices: a whole 4x8x8 slice. The times are simulated.
512 devices in a mesh: seg: 128 (over y, z, core), head: 4 (over x).
Axes of the slice: x: 4, y: 8, z: 8, core: 2. Of those that a mesh axis runs over, the one named last changes fastest.
Arguments:
- inputs: bfloat16 [256, 512, 1024], P('seg', None, 'head'), may hold values from -0.25 to 0.25
- cotangent: bfloat16 [256, 512, 1024], P('seg', None, 'head'), may hold values from -0.25 to 0.25
- state_in: bfloat16 [256, 512, 128], P('seg'), may hold values from -1.75 to 1.75
- state_out: bfloat16 [256, 512, 128], P('seg'), may hold values from -1.75 to 1.75
- log_decay: float32 [256, 16, 512], P('seg', 'head'), may hold values from -1 to 0
- parents: int32 [256], replicated, may hold values from -1 to 7, as said below
- slot_segment: int32 [256], replicated, may hold values from 0 to 255, as said below
Outputs:
- grad_inputs: bfloat16 [256, 512, 1024], P('seg', None, 'head')
- grad_state_in: float32 [256, 512, 128], P('seg', 'head')
- grad_state_out: float32 [256, 512, 128], P('seg', 'head')
Inputs may be any that keep to these rules, and one draw needn't show every extreme that they name: parents[s] is -1 for s < 2; each of the next 6 segments has a parent below 2; every other segment has a parent from 2 to 7; every segment below 8 has a child. `slot_segment`: each segment is held in exactly one slot.
All inputs are finite; a program needn't handle non-finite values.
Results may differ from a plain program's by a relative error of at most 0.0085.
Values sent between devices are 32-bit elements; how exact they have to be, the bound alone decides.
A program may use at most 64 MiB of HBM per device.

v0:
```python
import jax
import jax.numpy as jnp
from jax import lax
from jax.sharding import PartitionSpec as P

ROOTS = 2
MIDS = 6


def causal_decay(cumulative):
    length = cumulative.shape[1]
    later = jnp.arange(length)[:, None] >= jnp.arange(length)[None, :]
    spread = cumulative[:, :, None] - cumulative[:, None, :]
    return jnp.where(later[None], jnp.exp(jnp.where(later[None], spread, 0.0)), 0.0)


def local_terms(sliced):
    inputs_s, cotan_s, sin_s, sout_s, decay_s = sliced
    length = inputs_s.shape[0]
    head_count = decay_s.shape[0]
    head_width = inputs_s.shape[1] // head_count
    cumulative = jnp.cumsum(decay_s, axis=1)
    to_end = jnp.exp(cumulative[:, -1:] - cumulative)
    from_start = jnp.exp(cumulative)
    input_heads = inputs_s.reshape(length, head_count, head_width)
    cotan_heads = cotan_s.reshape(length, head_count, head_width)
    scaled_in = (input_heads.astype(jnp.float32) * to_end.T[:, :, None]).astype(jnp.bfloat16)
    scaled_cot = (cotan_heads.astype(jnp.float32) * from_start.T[:, :, None]).astype(jnp.bfloat16)
    local_end = jnp.einsum("lhp,ln->hpn", scaled_in, sin_s, preferred_element_type=jnp.float32)
    local_adj = jnp.einsum("lhp,ln->hpn", scaled_cot, sout_s, preferred_element_type=jnp.float32)
    scores = jnp.dot(sout_s, sin_s.T, preferred_element_type=jnp.float32)
    decay_mask = causal_decay(cumulative)
    weights = (decay_mask * scores[None]).astype(jnp.bfloat16)
    quad_in = jnp.einsum("htu,thp->uhp", weights, cotan_heads, preferred_element_type=jnp.float32)
    products = jnp.einsum(
        "thp,uhp->htu", cotan_heads, input_heads, preferred_element_type=jnp.float32
    )
    coupled = (decay_mask * products).astype(jnp.bfloat16)
    write_quad = jnp.einsum("htu,tn->un", coupled, sout_s, preferred_element_type=jnp.float32)
    read_quad = jnp.einsum("htu,un->tn", coupled, sin_s, preferred_element_type=jnp.float32)
    return (quad_in, write_quad, read_quad, local_end, local_adj, to_end, from_start)


def gather_rows(flags, states):
    return jnp.einsum("sk,shpn->khpn", flags, states, precision=lax.Precision.HIGHEST)


def spread_rows(flags, table):
    return jnp.einsum("sk,khpn->shpn", flags, table, precision=lax.Precision.HIGHEST)


def split_product(form, data, table):
    upper = table.astype(jnp.bfloat16)
    lower = (table - upper.astype(jnp.float32)).astype(jnp.bfloat16)
    first = jnp.einsum(form, data, upper, preferred_element_type=jnp.float32)
    return first + jnp.einsum(form, data, lower, preferred_element_type=jnp.float32)


def shards(inputs, cotangent, state_in, state_out, log_decay, parents, slot_segment):
    seg_dev = inputs.shape[0]
    length = inputs.shape[1]
    head_count = log_decay.shape[1]
    head_width = inputs.shape[2] // head_count
    slot_count = slot_segment.shape[0]
    quad_in, write_quad, read_quad, local_end, local_adj, to_end, from_start = lax.map(
        local_terms, (inputs, cotangent, state_in, state_out, log_decay)
    )
    end_decay = jnp.exp(jnp.sum(log_decay, axis=2))
    decay_four = end_decay[:, :, None, None]
    first_slot = lax.axis_index("seg") * seg_dev
    owned_ids = lax.dynamic_slice_in_dim(slot_segment, first_slot, seg_dev)
    everyone = jnp.arange(slot_count, dtype=jnp.int32)
    owned_parent = jnp.sum(
        jnp.where(owned_ids[:, None] == everyone[None, :], parents[None, :], 0), axis=1
    )
    parent_count = ROOTS + MIDS
    parent_ids = jnp.arange(parent_count, dtype=jnp.int32)
    holds_row = (owned_ids[:, None] == parent_ids[None, :]).astype(jnp.float32)
    child_of = (owned_parent[:, None] == parent_ids[None, :]).astype(jnp.float32)
    root_table = lax.psum(gather_rows(holds_row[:, :ROOTS], local_end), "seg")
    start_mid = spread_rows(child_of[:, :ROOTS], root_table)
    mid_table = lax.psum(
        gather_rows(holds_row[:, ROOTS:], decay_four * start_mid + local_end), "seg"
    )
    start_state = start_mid + spread_rows(child_of[:, ROOTS:], mid_table)
    mid_adj = lax.psum(gather_rows(child_of[:, ROOTS:], local_adj), "seg")
    end_mid = spread_rows(holds_row[:, ROOTS:], mid_adj)
    root_adj = lax.psum(gather_rows(child_of[:, :ROOTS], local_adj + decay_four * end_mid), "seg")
    adjoint_end = end_mid + spread_rows(holds_row[:, :ROOTS], root_adj)
    input_heads = inputs.reshape(seg_dev, length, head_count, head_width)
    cotan_heads = cotangent.reshape(seg_dev, length, head_count, head_width)
    end_weight = jnp.transpose(to_end, (0, 2, 1))
    start_weight = jnp.transpose(from_start, (0, 2, 1))
    state_in_term = end_weight[..., None] * split_product("sun,shpn->suhp", state_in, adjoint_end)
    grad_inputs = (
        (quad_in + state_in_term)
        .astype(jnp.bfloat16)
        .reshape(seg_dev, length, head_count * head_width)
    )
    write_state = jnp.sum(
        end_weight[..., None] * split_product("suhp,shpn->suhn", input_heads, adjoint_end), axis=2
    )
    read_state = jnp.sum(
        start_weight[..., None] * split_product("sthp,shpn->sthn", cotan_heads, start_state), axis=2
    )
    grad_state_in, grad_state_out = (
        lax.psum_scatter(write_quad + write_state, "head", scatter_dimension=1, tiled=True),
        lax.psum_scatter(read_quad + read_state, "head", scatter_dimension=1, tiled=True),
    )
    return (grad_inputs, grad_state_in, grad_state_out)


def solution(mesh):
    placed = (
        P("seg", None, "head"),
        P("seg", None, "head"),
        P("seg", None, None),
        P("seg", None, None),
        P("seg", "head", None),
        P(),
        P(),
    )
    return jax.shard_map(
        shards,
        mesh=mesh,
        in_specs=placed,
        out_specs=(P("seg", None, "head"), P("seg", "head", None), P("seg", "head", None)),
        check_vma=False,
    )
```

profile of v0, /device:TPU:1, one launch (start us, length us, event | category | flops | bytes accessed | tf_op | source)
XLA Modules:
  0.0 518.4 jit_solution(13523198974815908978)
XLA Ops:
  7.3 0.8 dynamic_slice.21
  8.2 0.9 fusion.49
  9.1 1.3 copy.88
  10.4 1.3 copy.87
  11.6 32.4 %while.22 = (s32[]{:T(128)}, f32[2,512,4,64]{1,3,2,0:T(8,128)}, f32[2,512,128]{1,2,0:T(8,128)}, f32[2,512,128]{1,2,0:T(8,128)S(1)}, f32[2,4,64,128]{3,0,2,1:T(2,...) while((s32[]{:T(128)}, f32[2,512,4,64]{1,3,2,0:T(8,128)}, ...), condition=%wide.region_4.5_spmd, body=%wide.region_0.4_spmd.sunk | while | flops 550508608 | bytes 22753060 | solution.py:65
  11.7 0.7 constant_dynamic-slice_fusion.6
  12.4 1.2 reduce-window.12
  14.3 0.7 exponential_dynamic-update-slice_fusion.3
  15.5 2.6 dynamic_update_slice.40
  18.3 4.2 dynamic_update_slice.41
  22.5 1.5 convert_reduce_fusion.2
  24.0 0.3 fusion.134
  24.6 0.3 fusion.131
  25.2 1.6 fusion.132
  26.8 1.0 copy-done.3
  27.9 0.7 constant_dynamic-slice_fusion.6
  28.6 1.2 reduce-window.12
  30.5 0.7 exponential_dynamic-update-slice_fusion.3
  31.7 2.6 dynamic_update_slice.40
  34.6 4.2 dynamic_update_slice.41
  38.7 1.5 convert_reduce_fusion.2
  40.2 0.3 fusion.134
  41.4 1.6 fusion.132
  43.1 1.0 copy-done.3
  44.1 1.4 fusion.50
  45.5 2.8 fusion.59
  48.3 0.8 reduce_sum.50
  49.2 202.2 %all-reduce.7.cloned.1.call-done = (f32[6,4,64,128]{3,0,2,1:T(8,128)}, f32[2,4,64,128]{3,0,2,1:T(2,128)}) async-done(((f32[6,4,64,128]{3,0,2,1:T(8,128)}, f32[2,4,64,128]{3,0,2,1:T(2,128)}), (f32[6,4,64,128]{3,0,2,1:T(8,128)}, f32[2,4,64,128]{3,0,2,1:T(2,128)})) %all-reduce.7.cloned.1.call-update) | async-done | bytes 1048592 | tf_op jit(solution)/shard_map/psum | solution.py:86
  251.4 1.8 fusion.55
  253.3 1.5 fusion.61
  254.8 1.6 fusion.41
  256.4 1.8 fusion.38
  258.5 195.1 %all-reduce.5.cloned.1.call-done = (f32[2,4,64,128]{3,0,2,1:T(2,128)}, f32[6,4,64,128]{3,0,2,1:T(8,128)}) async-done(((f32[2,4,64,128]{3,0,2,1:T(2,128)}, f32[6,4,64,128]{3,0,2,1:T(8,128)}), (f32[2,4,64,128]{3,0,2,1:T(2,128)}, f32[6,4,64,128]{3,0,2,1:T(8,128)})) %all-reduce.5.cloned.1.call-update) | async-done | bytes 1048592 | tf_op jit(solution)/shard_map/psum | solution.py:88
  453.6 1.5 fusion.52
  455.2 0.5 fusion.72
  455.7 1.4 fusion.30
  457.1 0.9 add.65
  458.1 0.6 fusion.57
  458.7 0.5 fusion.47
  459.2 1.3 fusion.29
  460.6 0.9 add.70
  461.5 0.3 fusion.36
  462.0 1.0 fusion.34
  463.0 1.0 copy.104
  464.0 17.0 %reduce-scatter.3.cloned.1.call-done = f32[2,128,128]{1,2,0:T(8,128)} async-done(((f32[2,512,128]{1,2,0:T(8,128)}), f32[2,128,128]{1,2,0:T(8,128)}) %reduce-scatter.3.cloned.1.call-update) | async-done | bytes 131088 | tf_op jit(solution)/shard_map/reduce_scatter | solution.py:107
  481.0 1.7 copy.105
  482.6 27.6 %reduce-scatter.5.cloned.1.call-done = f32[2,128,128]{1,2,0:T(8,128)} async-done(((f32[2,512,128]{1,2,0:T(8,128)}), f32[2,128,128]{1,2,0:T(8,128)}) %reduce-scatter.5.cloned.1.call-update) | async-done | bytes 131088 | tf_op jit(solution)/shard_map/reduce_scatter | solution.py:108
  510.2 1.7 copy.106
  (81 shorter events, 5.3 us)
Async XLA Ops:
  7.2 4.5 copy-start
  7.2 4.5 copy-start.1
  7.2 244.2 %all-reduce.7.cloned.1.call-start = ((), (), s32[]{:S(2)}) async-start(), calls=%async_computation.5 | async-start | bytes 2621440 | tf_op jit(solution)/shard_map/psum | solution.py:86
  22.5 1.8 copy-start.8
  24.0 1.2 copy-start.2
  24.6 2.2 copy-start.9
  26.8 1.0 copy-start.3
  38.7 1.8 copy-start.8
  40.2 1.2 copy-start.2
  40.8 2.2 copy-start.9
  43.0 1.0 copy-start.3
  44.1 209.2 %copy-start.6 = (f32[2,512,128]{1,2,0:T(8,128)}, f32[2,512,128]{1,2,0:T(8,128)S(1)}, u32[]{:S(2)}) copy-start(f32[2,512,128]{1,2,0:T(8,128)S(1)} %get-tuple-element.80) | copy-start | bytes 1572868
  45.5 209.3 %copy-start.11 = (f32[2,4,64,128]{3,0,2,1:T(2,128)S(1)}, f32[2,4,64,128]{3,0,2,1:T(2,128)}, u32[]{:S(2)}) copy-start(f32[2,4,64,128]{3,0,2,1:T(2,128)} %get-tuple-element.78) | copy-start | bytes 786436
  48.3 405.3 %all-reduce.5.cloned.1.call-start = ((), (), s32[]{:S(2)}) async-start(), calls=%async_computation.4 | async-start | bytes 2621440 | tf_op jit(solution)/shard_map/psum | solution.py:88
  258.2 222.7 %reduce-scatter.3.cloned.1.call-start = ((), (), s32[]{:S(2)}) async-start(), calls=%async_computation.2 | async-start | bytes 655360 | tf_op jit(solution)/shard_map/reduce_scatter | solution.py:107
  455.7 1.4 copy-start.10
  455.7 2.4 copy-start.5
  458.0 52.2 %reduce-scatter.5.cloned.1.call-start = ((), (), s32[]{:S(2)}) async-start(), calls=%async_computation.3 | async-start | bytes 655360 | tf_op jit(solution)/shard_map/reduce_scatter | solution.py:108
  459.2 1.4 copy-start.7
  460.6 1.4 copy-start.4
Sparse Core Ops, SparseCore 0:
  48.4 202.9 all-reduce.6
  258.4 195.1 all-reduce.4
  458.1 22.7 reduce-scatter.2
  483.7 26.5 reduce-scatter.4
where the time goes:
time: 520 us; the launch traced here: 518 us
  waiting for transfers between devices  442 us (85%)
  matrix products  26.9 us (5%)
  local copies, waits for them, and re-layouts  26.4 us (5%)
  between operations  14 us (3%)
  other arithmetic  8.66 us (2%)
    psum x1, waiting for transfers between devices, shards(): mid_adj = lax.psum(gather_rows(child_of[:, ROOTS:], local_adj), 'seg')  202 us
    psum x1, waiting for transfers between devices, shards(): lax.psum(gather_rows(child_of[:, :ROOTS], local_adj + decay_four * end_mi...  195 us
    reduce_scatter x1, waiting for transfers between devices, shards(): lax.psum_scatter(read_quad + read_state, 'head', scatter_dimension=1, til...  27.6 us
    reduce_scatter x1, waiting for transfers between devices, shards(): lax.psum_scatter(write_quad + write_state, 'head', scatter_dimension=1, t...  17 us
    dynamic_update_slice x4, local copies, waits for them, and re-layouts, shards(): lax.map(local_terms, (inputs, cotangent, state_in, state_out, log_decay))  13.6 us
  transfers between devices with their start and end apart: 4, of which 4 were waited for; matrix products, arithmetic and copies ran while one was open for 2% of the time, Pallas kernels for 0%

commit v1 on v0

v1 whole, which is shorter than its diff:
```python
import jax
import jax.numpy as jnp
from jax import lax
from jax.experimental import pallas as pl
from jax.experimental.pallas import tpu as pltpu
from jax.sharding import PartitionSpec as P

MESH = pl.DeviceIdType.MESH
F32 = jnp.float32
BF16 = jnp.bfloat16

ROOTS = 2
TABLE = 8
RING = 8
CORES = 2
HEAD_DEVS = 4
SEG_DEV = 2
LENGTH = 512
HEADS_DEV = 4
HEAD_DIM = 64
WIDTH = HEADS_DEV * HEAD_DIM
STATE = 128
SLICE = STATE // RING
BLOCK = 128


def dot(a, b):
    return jnp.dot(a, b, preferred_element_type=F32)


def dot_nt(a, b):
    return lax.dot_general(a, b, (((1,), (1,)), ((), ())), preferred_element_type=F32)


def dot_tn(a, b):
    return lax.dot_general(a, b, (((0,), (0,)), ((), ())), preferred_element_type=F32)


def seg_index(y, z, c):
    return (y * RING + z) * CORES + c


def split(value):
    upper = value.astype(BF16)
    return upper, (value - upper.astype(F32)).astype(BF16)


def kernel(
    inputs, cotan, sin, sout, ldec, parents, slots,
    grad_in, grad_sin, grad_sout,
    cum_row, cum_col, weight_end, scaled_in, scaled_cot, quad_in, part,
    send1f, recv1f, send1j, recv1j, send2f, recv2f, send2j, recv2j,
    send3, recv3, table, send4, recv4, recvx,
    ss1, rs1, ss2, rs2, ss3, rs3, ss4, rs4, ssx, rsx,
):
    s = lax.axis_index("seg")
    x = lax.axis_index("head")
    c = lax.rem(s, CORES)
    z = lax.rem(s // CORES, RING)
    y = s // (CORES * RING)

    mine = (y, z)
    other = (z, y)

    def first_peer(half, i):
        if half == 0:
            return seg_index(lax.rem(y + i, RING), z, c)
        return seg_index(y, lax.rem(z + i, RING), c)

    def second_peer(half, i, k):
        ck = lax.rem(c + k, CORES)
        if half == 0:
            return seg_index(y, lax.rem(z + i, RING), ck)
        return seg_index(lax.rem(y + i, RING), z, ck)

    def source_seg(half, i):
        if half == 0:
            return seg_index(lax.rem(y + RING - i, RING), z, c)
        return seg_index(y, lax.rem(z + RING - i, RING), c)

    barrier = pltpu.get_barrier_semaphore()
    peers = []
    for half in range(2):
        for i in range(1, RING):
            for k in range(CORES):
                peers.append((second_peer(half, i, k), x))
    peers.append((seg_index(y, z, lax.rem(c + 1, CORES)), x))
    for i in range(1, HEAD_DEVS):
        peers.append((s, lax.rem(x + i, HEAD_DEVS)))
    for peer in peers:
        pl.semaphore_signal(barrier, inc=1, device_id=peer, device_id_type=MESH)

    copies = []

    def send(src, dst, ssem, rsem, peer):
        copy = pltpu.make_async_remote_copy(
            src_ref=src, dst_ref=dst, send_sem=ssem, recv_sem=rsem,
            device_id=peer, device_id_type=MESH,
        )
        copy.start()
        copies.append(copy)
        return copy

    rows = SEG_DEV * HEADS_DEV
    blocks = LENGTH // BLOCK
    decay = jnp.concatenate([ldec[q] for q in range(SEG_DEV)], axis=0)
    stacked = jnp.concatenate([decay[:, b * BLOCK : (b + 1) * BLOCK] for b in range(blocks)], axis=0)
    top, rest = stacked.astype(BF16), None
    rest = stacked - top.astype(F32)
    middle, low = split(rest)
    earlier = lax.broadcasted_iota(jnp.int32, (BLOCK, BLOCK), 0)
    later = lax.broadcasted_iota(jnp.int32, (BLOCK, BLOCK), 1)
    causal = earlier <= later
    ones = jnp.where(causal, 1.0, 0.0).astype(BF16)
    sums = dot(low, ones) + dot(middle, ones) + dot(top, ones)
    base = jnp.zeros((rows, 1), F32)
    pieces = []
    for b in range(blocks):
        piece = sums[b * rows : (b + 1) * rows] + base
        pieces.append(piece)
        base = piece[:, BLOCK - 1 : BLOCK]
    cumulative = jnp.concatenate(pieces, axis=1)
    cum_row[...] = cumulative
    columns = jnp.concatenate(
        [jnp.exp(base - cumulative), jnp.exp(cumulative), cumulative, jnp.zeros_like(cumulative)], axis=0
    )
    columns = jnp.transpose(columns)
    cum_col[...] = columns
    upper, lower = split(columns)
    key_row = lax.broadcasted_iota(jnp.int32, (4 * rows, 2 * WIDTH), 0)
    key_lane = lax.broadcasted_iota(jnp.int32, (4 * rows, 2 * WIDTH), 1)
    for q in range(SEG_DEV):
        wanted = (key_lane // WIDTH) * rows + q * HEADS_DEV + lax.rem(key_lane, WIDTH) // HEAD_DIM
        pick = jnp.where(key_row == wanted, 1.0, 0.0).astype(BF16)
        spread = dot(upper, pick) + dot(lower, pick)
        to_end, from_start = spread[:, :WIDTH], spread[:, WIDTH:]
        weight_end[q] = to_end
        s_in = (inputs[q].astype(F32) * to_end).astype(BF16)
        s_cot = (cotan[q].astype(F32) * from_start).astype(BF16)
        scaled_in[q] = s_in
        scaled_cot[q] = s_cot
        local_end = dot_tn(sin[q], s_in)
        local_adj = dot_tn(sout[q], s_cot)
        end_decay = from_start[LENGTH - 1 : LENGTH]
        for half in range(2):
            lanes = slice(half * BLOCK, (half + 1) * BLOCK)
            place = pl.ds(q * SLICE, SLICE)
            send1f[half, :, place, :] = local_end[:, lanes].reshape(RING, SLICE, BLOCK)
            send1j[half, :, place, :] = local_adj[:, lanes].reshape(RING, SLICE, BLOCK)
            tile = jnp.broadcast_to(end_decay[:, lanes].reshape(1, 1, BLOCK), (RING, 8, BLOCK))
            send1f[half, :, pl.ds(SEG_DEV * SLICE + 8 * q, 8), :] = tile

    pl.semaphore_wait(barrier, len(peers))

    got1 = []
    for chunk, (out, into) in enumerate(((send1f, recv1f), (send1j, recv1j))):
        for i in range(1, RING):
            for half in range(2):
                to = lax.rem(mine[half] + i, RING)
                got1.append((chunk, send(
                    out.at[half, to], into.at[half, i],
                    ss1.at[chunk, half, i], rs1.at[chunk, half, i], (first_peer(half, i), x),
                )))
    for half in range(2):
        recv1f[half, 0] = send1f[half, mine[half]]
        recv1j[half, 0] = send1j[half, mine[half]]

    lane = lax.broadcasted_iota(jnp.int32, (BLOCK, BLOCK), 1)
    first_head = lane < HEAD_DIM
    for q in range(SEG_DEV):
        for b in range(blocks):
            u0 = b * BLOCK
            length = LENGTH - u0
            here = pl.ds(u0, BLOCK)
            onward = pl.ds(u0, length)
            sin_b = sin[q, here]
            sout_b = sout[q, onward]
            scores = dot_nt(sin_b, sout_b)
            coupled = None
            for pair in range(HEADS_DEV // 2):
                lanes = pl.ds(pair * BLOCK, BLOCK)
                in_pair = inputs[q, here, lanes]
                cot_pair = cotan[q, onward, lanes]
                results = []
                for k in range(2):
                    r = q * HEADS_DEV + pair * 2 + k
                    col = 2 * rows + r
                    spread = cum_row[r : r + 1, onward] - cum_col[here, col : col + 1]
                    mask = jnp.where(causal, jnp.exp(jnp.where(causal, spread[:, :BLOCK], 0.0)), 0.0)
                    if length > BLOCK:
                        mask = jnp.concatenate([mask, jnp.exp(spread[:, BLOCK:])], axis=1)
                    weights = (mask * scores).astype(BF16)
                    results.append(dot(weights, cot_pair))
                    own = first_head if k == 0 else jnp.logical_not(first_head)
                    in_head = jnp.where(own, in_pair.astype(F32), 0.0).astype(BF16)
                    term = mask * dot_nt(in_head, cot_pair)
                    coupled = term if coupled is None else coupled + term
                quad_in[q, here, lanes] = jnp.where(first_head, results[0], results[1])
            coupled = coupled.astype(BF16)
            part[0, q, here] = dot(coupled, sout_b)
            read = dot_tn(coupled, sin_b)
            if b == 0:
                part[1, q] = read
            else:
                part[1, q, onward] = part[1, q, onward] + read

    rank = lax.broadcasted_iota(jnp.int32, (TABLE, SLICE, BLOCK), 0)
    rank_row = lax.broadcasted_iota(jnp.int32, (TABLE, BLOCK), 0)
    got2 = []
    for chunk in range(2):
        for owner, copy in got1:
            if owner == chunk:
                copy.wait_recv()
        for half in range(2):
            total = jnp.zeros((TABLE, SLICE, BLOCK), F32)
            decays = jnp.zeros((TABLE, BLOCK), F32)
            for i in range(RING):
                for q in range(SEG_DEV):
                    segment = slots[source_seg(half, i) * SEG_DEV + q]
                    place = pl.ds(q * SLICE, SLICE)
                    if chunk == 0:
                        total = total + jnp.where(rank == segment, recv1f[half, i, place][None], 0.0)
                        row = recv1f[half, i, pl.ds(SEG_DEV * SLICE + 8 * q, 8)]
                        decays = decays + jnp.where(rank_row == segment, row, 0.0)
                    else:
                        parent = parents[segment]
                        total = total + jnp.where(rank == parent, recv1j[half, i, place][None], 0.0)
            out = send2f if chunk == 0 else send2j
            for k in range(TABLE):
                out[half, :, k, :] = total[k]
            if chunk == 0:
                out[half, :, pl.ds(TABLE, TABLE), :] = jnp.broadcast_to(
                    decays[None], (SLICE, TABLE, BLOCK)
                )
        out, into = ((send2f, recv2f), (send2j, recv2j))[chunk]
        for i in range(RING):
            for k in range(CORES):
                for half in range(2):
                    to = lax.rem(other[half] + i, RING) * CORES + lax.rem(c + k, CORES)
                    slot = i * CORES + k
                    if slot == 0:
                        into[half, 0] = out[half, to]
                        continue
                    got2.append((chunk, send(
                        out.at[half, to], into.at[half, slot],
                        ss2.at[chunk, half, slot], rs2.at[chunk, half, slot],
                        (second_peer(half, i, k), x),
                    )))

    got3 = []
    decays = [None, None]
    for chunk in range(2):
        for owner, copy in got2:
            if owner == chunk:
                copy.wait_recv()
        for half in range(2):
            into = recv2f if chunk == 0 else recv2j
            total = into[half, 0]
            for slot in range(1, SLICE):
                total = total + into[half, slot]
            if chunk == 0:
                decays[half] = total[TABLE:]
                carried = jnp.zeros((TABLE, BLOCK), F32)
                for m in range(ROOTS, TABLE):
                    start = jnp.where(parents[m] == 0, total[0:1], total[1:2])
                    carried = carried + jnp.where(rank_row == m, start, 0.0)
                send3[chunk, half] = total[:TABLE] + decays[half] * carried
            else:
                carried = jnp.zeros((TABLE, BLOCK), F32)
                product = decays[half] * total
                for m in range(ROOTS, TABLE):
                    carried = carried + jnp.where(rank_row == parents[m], product[m : m + 1], 0.0)
                send3[chunk, half] = total + jnp.where(rank_row < ROOTS, carried, 0.0)
        for i in range(RING):
            for k in range(CORES):
                for half in range(2):
                    row = other[half] * CORES + c
                    slot = i * CORES + k
                    if slot == 0:
                        recv3[chunk, half, row] = send3[chunk, half]
                        continue
                    got3.append((chunk, send(
                        send3.at[chunk, half], recv3.at[chunk, half, row],
                        ss3.at[chunk, half, slot], rs3.at[chunk, half, slot],
                        (second_peer(half, i, k), x),
                    )))

    got4 = []
    for chunk in range(2):
        for owner, copy in got3:
            if owner == chunk:
                copy.wait_recv()
        for half in range(2):
            for k in range(TABLE):
                table[chunk, half, k] = recv3[chunk, half, :, k, :]
            for i in range(RING):
                to = lax.rem(mine[half] + i, RING)
                for q in range(SEG_DEV):
                    segment = slots[first_peer(half, i) * SEG_DEV + q]
                    if chunk == 0:
                        index = parents[segment]
                        exists = index >= 0
                        index = jnp.maximum(index, 0)
                    else:
                        exists = segment < TABLE
                        index = jnp.minimum(segment, TABLE - 1)
                    picked = table[chunk, half, index]
                    send4[chunk, half, i, q] = jnp.where(exists, picked, 0.0)
        for i in range(RING):
            for half in range(2):
                row = mine[half]
                if i == 0:
                    recv4[chunk, half, row] = send4[chunk, half, 0]
                    continue
                got4.append((chunk, send(
                    send4.at[chunk, half, i], recv4.at[chunk, half, row],
                    ss4.at[chunk, half, i], rs4.at[chunk, half, i], (first_peer(half, i), x),
                )))

    gotx = []
    for chunk in range(2):
        for owner, copy in got4:
            if owner == chunk:
                copy.wait_recv()
        kind = 1 - chunk
        states = []
        for q in range(SEG_DEV):
            halves = [recv4[chunk, half, :, q].reshape(STATE, BLOCK) for half in range(2)]
            state = jnp.concatenate(halves, axis=1).astype(BF16)
            states.append(state)
            data = scaled_cot[q] if chunk == 0 else scaled_in[q]
            part[kind, q] = part[kind, q] + dot_nt(data, state)
        for i in range(1, HEAD_DEVS):
            to = lax.rem(x + i, HEAD_DEVS)
            piece = pl.ds(pl.multiple_of(to * BLOCK, BLOCK), BLOCK)
            gotx.append((chunk, send(
                part.at[kind, :, piece], recvx.at[kind, i], ssx.at[kind, i], rsx.at[kind, i], (s, to)
            )))
        if chunk == 1:
            for q in range(SEG_DEV):
                term = weight_end[q] * dot(sin[q], states[q])
                grad_in[q] = (quad_in[q] + term).astype(BF16)
    own = pl.ds(pl.multiple_of(x * BLOCK, BLOCK), BLOCK)
    for chunk in range(2):
        for owner, copy in gotx:
            if owner == chunk:
                copy.wait_recv()
        kind = 1 - chunk
        total = part[kind, :, own]
        for i in range(1, HEAD_DEVS):
            total = total + recvx[kind, i]
        result = grad_sin if kind == 0 else grad_sout
        result[...] = total
    for copy in copies:
        copy.wait_send()


def shards(inputs, cotangent, state_in, state_out, log_decay, parents, slot_segment):
    vmem = pl.BlockSpec(memory_space=pltpu.VMEM)
    smem = pl.BlockSpec(memory_space=pltpu.SMEM)
    both = SEG_DEV * HEADS_DEV
    slots2 = RING * CORES
    dma = pltpu.SemaphoreType.DMA
    return pl.pallas_call(
        kernel,
        out_shape=(
            jax.ShapeDtypeStruct(inputs.shape, BF16),
            jax.ShapeDtypeStruct((SEG_DEV, BLOCK, STATE), F32),
            jax.ShapeDtypeStruct((SEG_DEV, BLOCK, STATE), F32),
        ),
        in_specs=[vmem] * 5 + [smem] * 2,
        out_specs=(vmem, vmem, vmem),
        scratch_shapes=[
            pltpu.VMEM((both, LENGTH), F32),
            pltpu.VMEM((LENGTH, 4 * both), F32),
            pltpu.VMEM((SEG_DEV, LENGTH, WIDTH), F32),
            pltpu.VMEM((SEG_DEV, LENGTH, WIDTH), BF16),
            pltpu.VMEM((SEG_DEV, LENGTH, WIDTH), BF16),
            pltpu.VMEM((SEG_DEV, LENGTH, WIDTH), F32),
            pltpu.VMEM((2, SEG_DEV, LENGTH, STATE), F32),
            pltpu.VMEM((2, RING, SEG_DEV * (SLICE + 8), BLOCK), F32),
            pltpu.VMEM((2, RING, SEG_DEV * (SLICE + 8), BLOCK), F32),
            pltpu.VMEM((2, RING, SEG_DEV * SLICE, BLOCK), F32),
            pltpu.VMEM((2, RING, SEG_DEV * SLICE, BLOCK), F32),
            pltpu.VMEM((2, SLICE, 2 * TABLE, BLOCK), F32),
            pltpu.VMEM((2, slots2, 2 * TABLE, BLOCK), F32),
            pltpu.VMEM((2, SLICE, TABLE, BLOCK), F32),
            pltpu.VMEM((2, slots2, TABLE, BLOCK), F32),
            pltpu.VMEM((2, 2, TABLE, BLOCK), F32),
            pltpu.VMEM((2, 2, SLICE, TABLE, BLOCK), F32),
            pltpu.VMEM((2, 2, TABLE, SLICE, BLOCK), F32),
            pltpu.VMEM((2, 2, RING, SEG_DEV, SLICE, BLOCK), F32),
            pltpu.VMEM((2, 2, RING, SEG_DEV, SLICE, BLOCK), F32),
            pltpu.VMEM((2, HEAD_DEVS, SEG_DEV, BLOCK, STATE), F32),
            dma((2, 2, RING)), dma((2, 2, RING)),
            dma((2, 2, slots2)), dma((2, 2, slots2)),
            dma((2, 2, slots2)), dma((2, 2, slots2)),
            dma((2, 2, RING)), dma((2, 2, RING)),
            dma((2, HEAD_DEVS)), dma((2, HEAD_DEVS)),
        ],
        compiler_params=pltpu.CompilerParams(
            collective_id=0, has_side_effects=True, vmem_limit_bytes=40 * 2**20
        ),
    )(inputs, cotangent, state_in, state_out, log_decay, parents, slot_segment)


def solution(mesh):
    placed = (
        P("seg", None, "head"),
        P("seg", None, "head"),
        P("seg", None, None),
        P("seg", None, None),
        P("seg", "head", None),
        P(),
        P(),
    )
    return jax.shard_map(
        shards,
        mesh=mesh,
        in_specs=placed,
        out_specs=(P("seg", None, "head"), P("seg", "head", None), P("seg", "head", None)),
        check_vma=False,
    )
```

time: 520 us -> 68.5 us (0.13)
  waiting for transfers between devices: 442 us -> 0 us
  Pallas kernels: 0 us -> 59.2 us
  matrix products: 26.9 us -> 0 us
  local copies, waits for them, and re-layouts: 26.4 us -> 8.15 us
  between operations: 14 us -> 0.66 us
  other arithmetic: 8.66 us -> 0 us
    psum x2 -> x0, waiting for transfers between devices: 397 us -> none  [the longest x1 202 us: shards(): mid_adj = lax.psum(gather_rows(child_of[:, ROOTS:], local_adj), 'seg')]
    pallas_call x0 -> x1, Pallas kernels: none -> 59.2 us  [shards(): pl.pallas_call(kernel, out_shape=(jax.ShapeDtypeStruct(inputs.shape, BF16...]
    reduce_scatter x2 -> x0, waiting for transfers between devices: 44.5 us -> none  [the longest x1 27.6 us: shards(): lax.psum_scatter(read_quad + read_state, 'head', scatter_dimension=1, til...]
    dot_general x28 -> x0, matrix products: 26.9 us -> none  [the longest x4 7.56 us: gather_rows(): jnp.einsum('sk,shpn->khpn', flags, states, precision=lax.Precision.HIGHEST)]
    dynamic_update_slice x4 -> x0, local copies, waits for them, and re-layouts: 13.6 us -> none  [shards(): lax.map(local_terms, (inputs, cotangent, state_in, state_out, log_decay))]
    while x22 -> x0, local copies, waits for them, and re-layouts: 5.36 us -> none
  transfers between devices with their start and end apart: 4 -> 0, of which waited for: 4 -> 0; matrix products, arithmetic and copies ran while one was open for 2% -> 0% of each run, Pallas kernels for 0% -> 0%
where the time goes in v1:
time: 68.5 us; the launch traced here: 68 us
  Pallas kernels  59.2 us (86%)
  local copies, waits for them, and re-layouts  8.15 us (12%)
    pallas_call x1, Pallas kernels, shards(): pl.pallas_call(kernel, out_shape=(jax.ShapeDtypeStruct(inputs.shape, BF16...  59.2 us
    unnamed x17, local copies, waits for them, and re-layouts  8.15 us

profile of v1, /device:TPU:1, one launch (start us, length us, event | category | flops | bytes accessed | tf_op | source)
XLA Modules:
  0.0 68.0 jit_solution(3970016443812496738)
XLA Ops:
  0.6 0.0 copy-start
  0.6 1.0 %copy-done = bf16[2,512,256]{2,1,0:T(8,128)(2,1)S(1)} copy-done((bf16[2,512,256]{2,1,0:T(8,128)(2,1)S(1)}, bf16[2,512,256]{2,1,0:T(8,128)(2,1)}, u32[]{:S(2)}) %copy-start) | copy-done | bytes 524312
  1.7 0.0 copy-start.1
  1.7 1.0 %copy-done.1 = bf16[2,512,256]{2,1,0:T(8,128)(2,1)S(1)} copy-done((bf16[2,512,256]{2,1,0:T(8,128)(2,1)S(1)}, bf16[2,512,256]{2,1,0:T(8,128)(2,1)}, u32[]{:S(2)}) %copy-start.1) | copy-done | bytes 524312
  2.7 0.0 copy-start.2
  2.7 0.9 %copy-done.2 = bf16[2,512,128]{2,1,0:T(8,128)(2,1)S(1)} copy-done((bf16[2,512,128]{2,1,0:T(8,128)(2,1)S(1)}, bf16[2,512,128]{2,1,0:T(8,128)(2,1)}, u32[]{:S(2)}) %copy-start.2) | copy-done | bytes 262168
  3.7 0.0 copy-start.3
  3.7 0.9 %copy-done.3 = bf16[2,512,128]{2,1,0:T(8,128)(2,1)S(1)} copy-done((bf16[2,512,128]{2,1,0:T(8,128)(2,1)S(1)}, bf16[2,512,128]{2,1,0:T(8,128)(2,1)}, u32[]{:S(2)}) %copy-start.3) | copy-done | bytes 262168
  4.6 0.0 copy-start.4
  4.6 0.7 %copy-done.4 = f32[2,4,512]{2,1,0:T(4,128)S(1)} copy-done((f32[2,4,512]{2,1,0:T(4,128)S(1)}, f32[2,4,512]{2,1,0:T(4,128)}, u32[]{:S(2)}) %copy-start.4) | copy-done | bytes 16408
  5.3 0.0 copy-start.5
  5.3 0.7 copy-done.5
  6.0 0.0 copy-start.6
  6.0 0.7 copy-done.6
  6.7 59.2 %shard_map.94 = (bf16[2,512,256]{2,1,0:T(8,128)(2,1)S(1)}, f32[2,128,128]{2,1,0:T(8,128)S(1)}, f32[2,128,128]{2,1,0:T(8,128)S(1)}) custom-call(bf16[2,512,256]{2,1,0:T(8,128)(2,1)S(1)} %copy-done, bf16[2,512,256]{2,1,0:T(8,128)(2,1)S(1)} %copy-done.1, bf16[2,512,128]{2,1,0:T(8,128)(2,1)S(1)} %copy-done.2, bf16[2,512,128]{2,1,0:T(8,128)(2,1)S(1)} %copy-done.3, ...), custom_call_target="tpu_custom_call" | custom-call | tf_op jit(solution)/shard_map/pallas_call | solution.py:364
  65.9 0.8 %copy.13 = bf16[2,512,256]{2,1,0:T(8,128)(2,1)} copy(bf16[2,512,256]{2,1,0:T(8,128)(2,1)S(1)} %get-tuple-element.6) | data formatting | bytes 1048576
  66.7 0.7 copy.14
  67.4 0.7 copy.15
Async XLA Ops:
  0.6 1.0 %copy-start = (bf16[2,512,256]{2,1,0:T(8,128)(2,1)S(1)}, bf16[2,512,256]{2,1,0:T(8,128)(2,1)}, u32[]{:S(2)}) copy-start(bf16[2,512,256]{2,1,0:T(8,128)(2,1)} %inputs.1) | copy-start | bytes 1572868
  1.7 1.0 %copy-start.1 = (bf16[2,512,256]{2,1,0:T(8,128)(2,1)S(1)}, bf16[2,512,256]{2,1,0:T(8,128)(2,1)}, u32[]{:S(2)}) copy-start(bf16[2,512,256]{2,1,0:T(8,128)(2,1)} %cotan.1) | copy-start | bytes 1572868
  2.7 0.9 %copy-start.2 = (bf16[2,512,128]{2,1,0:T(8,128)(2,1)S(1)}, bf16[2,512,128]{2,1,0:T(8,128)(2,1)}, u32[]{:S(2)}) copy-start(bf16[2,512,128]{2,1,0:T(8,128)(2,1)} %sin.1) | copy-start | bytes 786436
  3.7 0.9 %copy-start.3 = (bf16[2,512,128]{2,1,0:T(8,128)(2,1)S(1)}, bf16[2,512,128]{2,1,0:T(8,128)(2,1)}, u32[]{:S(2)}) copy-start(bf16[2,512,128]{2,1,0:T(8,128)(2,1)} %sout.1) | copy-start | bytes 786436
  4.6 0.7 %copy-start.4 = (f32[2,4,512]{2,1,0:T(4,128)S(1)}, f32[2,4,512]{2,1,0:T(4,128)}, u32[]{:S(2)}) copy-start(f32[2,4,512]{2,1,0:T(4,128)} %ldec.1) | copy-start | bytes 49156
  5.3 0.7 copy-start.5
  6.0 0.7 copy-start.6

commit v2 on v1

--- a/solution.py
+++ b/solution.py
@@ -22,6 +22,7 @@
 STATE = 128
 SLICE = STATE // RING
 BLOCK = 128
+ROW1 = SEG_DEV * SLICE
 
 
 def dot(a, b):
@@ -46,12 +47,13 @@
 
 
 def kernel(
-    inputs, cotan, sin, sout, ldec, parents, slots,
+    inputs_hbm, cotan_hbm, sin_hbm, sout_hbm, ldec_hbm, parents_hbm, slots_hbm,
     grad_in, grad_sin, grad_sout,
+    inputs, cotan, sin, sout, ldec, parents, slots, lsem,
     cum_row, cum_col, weight_end, scaled_in, scaled_cot, quad_in, part,
     send1f, recv1f, send1j, recv1j, send2f, recv2f, send2j, recv2j,
     send3, recv3, table, send4, recv4, recvx,
-    ss1, rs1, ss2, rs2, ss3, rs3, ss4, rs4, ssx, rsx,
+    out_in, out_sin, out_sout, sent, arrived, osem,
 ):
     s = lax.axis_index("seg")
     x = lax.axis_index("head")
@@ -77,6 +79,16 @@
         if half == 0:
             return seg_index(lax.rem(y + RING - i, RING), z, c)
         return seg_index(y, lax.rem(z + RING - i, RING), c)
+
+    loads = []
+    operands = (
+        (ldec_hbm, ldec), (inputs_hbm, inputs), (cotan_hbm, cotan), (sin_hbm, sin),
+        (sout_hbm, sout), (slots_hbm, slots), (parents_hbm, parents),
+    )
+    for n, (far, near) in enumerate(operands):
+        load = pltpu.make_async_copy(far, near, lsem.at[n])
+        load.start()
+        loads.append(load)
 
     barrier = pltpu.get_barrier_semaphore()
     peers = []
@@ -90,17 +102,23 @@
     for peer in peers:
         pl.semaphore_signal(barrier, inc=1, device_id=peer, device_id_type=MESH)
 
-    copies = []
-
-    def send(src, dst, ssem, rsem, peer):
+    pending = []
+
+    def send(src, dst, stage, peer):
+        pltpu.make_async_remote_copy(
+            src_ref=src, dst_ref=dst, send_sem=sent.at[stage], recv_sem=arrived.at[stage],
+            device_id=peer, device_id_type=MESH,
+        ).start()
+
+    def arrive(stage, whole):
         copy = pltpu.make_async_remote_copy(
-            src_ref=src, dst_ref=dst, send_sem=ssem, recv_sem=rsem,
-            device_id=peer, device_id_type=MESH,
+            src_ref=whole, dst_ref=whole, send_sem=sent.at[stage], recv_sem=arrived.at[stage],
+            device_id=(seg_index(y, z, lax.rem(c + 1, CORES)), x), device_id_type=MESH,
         )
-        copy.start()
-        copies.append(copy)
-        return copy
-
+        copy.wait_recv()
+        pending.append(copy)
+
+    loads[0].wait()
     rows = SEG_DEV * HEADS_DEV
     blocks = LENGTH // BLOCK
     decay = jnp.concatenate([ldec[q] for q in range(SEG_DEV)], axis=0)
@@ -127,8 +145,12 @@
     columns = jnp.transpose(columns)
     cum_col[...] = columns
     upper, lower = split(columns)
+    for load in loads[1:]:
+        load.wait()
     key_row = lax.broadcasted_iota(jnp.int32, (4 * rows, 2 * WIDTH), 0)
     key_lane = lax.broadcasted_iota(jnp.int32, (4 * rows, 2 * WIDTH), 1)
+    lane64 = lax.rem(lax.broadcasted_iota(jnp.int32, (1, WIDTH), 1), HEAD_DIM)
+    packed = None
     for q in range(SEG_DEV):
         wanted = (key_lane // WIDTH) * rows + q * HEADS_DEV + lax.rem(key_lane, WIDTH) // HEAD_DIM
         pick = jnp.where(key_row == wanted, 1.0, 0.0).astype(BF16)
@@ -141,28 +163,32 @@
         scaled_cot[q] = s_cot
         local_end = dot_tn(sin[q], s_in)
         local_adj = dot_tn(sout[q], s_cot)
-        end_decay = from_start[LENGTH - 1 : LENGTH]
+        segment = slots[s * SEG_DEV + q]
+        end_decay = jnp.where(lane64 == segment, from_start[LENGTH - 1 : LENGTH], 0.0)
+        packed = end_decay if q == 0 else packed + end_decay
         for half in range(2):
             lanes = slice(half * BLOCK, (half + 1) * BLOCK)
             place = pl.ds(q * SLICE, SLICE)
             send1f[half, :, place, :] = local_end[:, lanes].reshape(RING, SLICE, BLOCK)
             send1j[half, :, place, :] = local_adj[:, lanes].reshape(RING, SLICE, BLOCK)
-            tile = jnp.broadcast_to(end_decay[:, lanes].reshape(1, 1, BLOCK), (RING, 8, BLOCK))
-            send1f[half, :, pl.ds(SEG_DEV * SLICE + 8 * q, 8), :] = tile
+    for half in range(2):
+        row = packed[:, half * BLOCK : (half + 1) * BLOCK].reshape(1, 1, BLOCK)
+        send1f[half, :, pl.ds(ROW1, 1), :] = jnp.broadcast_to(row, (RING, 1, BLOCK))
 
     pl.semaphore_wait(barrier, len(peers))
 
-    got1 = []
-    for chunk, (out, into) in enumerate(((send1f, recv1f), (send1j, recv1j))):
+    rows1 = (pl.ds(0, ROW1 + 1), pl.ds(0, ROW1))
+    out1, in1 = (send1f, send1j), (recv1f, recv1j)
+    for chunk in range(2):
         for i in range(1, RING):
             for half in range(2):
                 to = lax.rem(mine[half] + i, RING)
-                got1.append((chunk, send(
-                    out.at[half, to], into.at[half, i],
-                    ss1.at[chunk, half, i], rs1.at[chunk, half, i], (first_peer(half, i), x),
-                )))
+                send(
+                    out1[chunk].at[half, to, rows1[chunk]], in1[chunk].at[half, i, rows1[chunk]],
+                    chunk, (first_peer(half, i), x),
+                )
     for half in range(2):
-        recv1f[half, 0] = send1f[half, mine[half]]
+        recv1f[half, 0, rows1[0]] = send1f[half, mine[half], rows1[0]]
         recv1j[half, 0] = send1j[half, mine[half]]
 
     lane = lax.broadcasted_iota(jnp.int32, (BLOCK, BLOCK), 1)
@@ -206,65 +232,66 @@
 
     rank = lax.broadcasted_iota(jnp.int32, (TABLE, SLICE, BLOCK), 0)
     rank_row = lax.broadcasted_iota(jnp.int32, (TABLE, BLOCK), 0)
-    got2 = []
-    for chunk in range(2):
-        for owner, copy in got1:
-            if owner == chunk:
-                copy.wait_recv()
+    rank_lane = lax.rem(lane[:TABLE], HEAD_DIM)
+    left = lane[:TABLE] < HEAD_DIM
+    rows2 = (pl.ds(0, TABLE + 1), pl.ds(0, TABLE))
+    out2, in2 = (send2f, send2j), (recv2f, recv2j)
+    decays = [None, None]
+
+    def second(chunk):
+        arrive(chunk, in1[chunk].at[:, pl.ds(1, RING - 1), rows1[chunk]])
+        out, into = out2[chunk], in2[chunk]
         for half in range(2):
             total = jnp.zeros((TABLE, SLICE, BLOCK), F32)
-            decays = jnp.zeros((TABLE, BLOCK), F32)
             for i in range(RING):
                 for q in range(SEG_DEV):
-                    segment = slots[source_seg(half, i) * SEG_DEV + q]
-                    place = pl.ds(q * SLICE, SLICE)
-                    if chunk == 0:
-                        total = total + jnp.where(rank == segment, recv1f[half, i, place][None], 0.0)
-                        row = recv1f[half, i, pl.ds(SEG_DEV * SLICE + 8 * q, 8)]
-                        decays = decays + jnp.where(rank_row == segment, row, 0.0)
-                    else:
-                        parent = parents[segment]
-                        total = total + jnp.where(rank == parent, recv1j[half, i, place][None], 0.0)
-            out = send2f if chunk == 0 else send2j
+                    index = slots[source_seg(half, i) * SEG_DEV + q]
+                    if chunk == 1:
+                        index = parents[index]
+                    block = in1[chunk][half, i, pl.ds(q * SLICE, SLICE)]
+                    total = total + jnp.where(rank == index, block[None], 0.0)
             for k in range(TABLE):
                 out[half, :, k, :] = total[k]
             if chunk == 0:
-                out[half, :, pl.ds(TABLE, TABLE), :] = jnp.broadcast_to(
-                    decays[None], (SLICE, TABLE, BLOCK)
+                row = recv1f[half, 0, pl.ds(ROW1, 1)]
+                for i in range(1, RING):
+                    row = row + recv1f[half, i, pl.ds(ROW1, 1)]
+                out[half, :, pl.ds(TABLE, 1), :] = jnp.broadcast_to(
+                    row.reshape(1, 1, BLOCK), (SLICE, 1, BLOCK)
                 )
-        out, into = ((send2f, recv2f), (send2j, recv2j))[chunk]
         for i in range(RING):
             for k in range(CORES):
                 for half in range(2):
                     to = lax.rem(other[half] + i, RING) * CORES + lax.rem(c + k, CORES)
                     slot = i * CORES + k
                     if slot == 0:
-                        into[half, 0] = out[half, to]
+                        into[half, 0, rows2[chunk]] = out[half, to, rows2[chunk]]
                         continue
-                    got2.append((chunk, send(
-                        out.at[half, to], into.at[half, slot],
-                        ss2.at[chunk, half, slot], rs2.at[chunk, half, slot],
-                        (second_peer(half, i, k), x),
-                    )))
-
-    got3 = []
-    decays = [None, None]
-    for chunk in range(2):
-        for owner, copy in got2:
-            if owner == chunk:
-                copy.wait_recv()
+                    send(
+                        out.at[half, to, rows2[chunk]], into.at[half, slot, rows2[chunk]],
+                        2 + chunk, (second_peer(half, i, k), x),
+                    )
+
+    def third(chunk):
+        into = in2[chunk]
+        arrive(2 + chunk, into.at[:, pl.ds(1, SLICE - 1), rows2[chunk]])
         for half in range(2):
-            into = recv2f if chunk == 0 else recv2j
-            total = into[half, 0]
+            total = into[half, 0, pl.ds(0, TABLE)]
             for slot in range(1, SLICE):
-                total = total + into[half, slot]
+                total = total + into[half, slot, pl.ds(0, TABLE)]
             if chunk == 0:
-                decays[half] = total[TABLE:]
+                row = into[half, 0, pl.ds(TABLE, 1)]
+                for slot in range(1, SLICE):
+                    row = row + into[half, slot, pl.ds(TABLE, 1)]
+                spread = jnp.where(rank_lane == rank_row, row, 0.0)
+                first = jnp.sum(jnp.where(left, spread, 0.0), axis=1, keepdims=True)
+                second_head = jnp.sum(jnp.where(left, 0.0, spread), axis=1, keepdims=True)
+                decays[half] = jnp.where(left, first, second_head)
                 carried = jnp.zeros((TABLE, BLOCK), F32)
                 for m in range(ROOTS, TABLE):
                     start = jnp.where(parents[m] == 0, total[0:1], total[1:2])
                     carried = carried + jnp.where(rank_row == m, start, 0.0)
-                send3[chunk, half] = total[:TABLE] + decays[half] * carried
+                send3[chunk, half] = total + decays[half] * carried
             else:
                 carried = jnp.zeros((TABLE, BLOCK), F32)
                 product = decays[half] * total
@@ -275,26 +302,20 @@
             for k in range(CORES):
                 for half in range(2):
                     row = other[half] * CORES + c
-                    slot = i * CORES + k
-                    if slot == 0:
+                    if i + k == 0:
                         recv3[chunk, half, row] = send3[chunk, half]
                         continue
-                    got3.append((chunk, send(
+                    send(
                         send3.at[chunk, half], recv3.at[chunk, half, row],
-                        ss3.at[chunk, half, slot], rs3.at[chunk, half, slot],
-                        (second_peer(half, i, k), x),
-                    )))
-
-    got4 = []
-    for chunk in range(2):
-        for owner, copy in got3:
-            if owner == chunk:
-                copy.wait_recv()
+                        4 + chunk, (second_peer(half, i, k), x),
+                    )
+
+    def fourth(chunk):
+        arrive(4 + chunk, recv3.at[chunk, :, pl.ds(0, SLICE - 1)])
         for half in range(2):
             for k in range(TABLE):
                 table[chunk, half, k] = recv3[chunk, half, :, k, :]
             for i in range(RING):
-                to = lax.rem(mine[half] + i, RING)
                 for q in range(SEG_DEV):
                     segment = slots[first_peer(half, i) * SEG_DEV + q]
                     if chunk == 0:
@@ -312,16 +333,13 @@
                 if i == 0:
                     recv4[chunk, half, row] = send4[chunk, half, 0]
                     continue
-                got4.append((chunk, send(
+                send(
                     send4.at[chunk, half, i], recv4.at[chunk, half, row],
-                    ss4.at[chunk, half, i], rs4.at[chunk, half, i], (first_peer(half, i), x),
-                )))
-
-    gotx = []
-    for chunk in range(2):
-        for owner, copy in got4:
-            if owner == chunk:
-                copy.wait_recv()
+                    6 + chunk, (first_peer(half, i), x),
+                )
+
+    def states_of(chunk):
+        arrive(6 + chunk, recv4.at[chunk, :, pl.ds(0, RING - 1)])
         kind = 1 - chunk
         states = []
         for q in range(SEG_DEV):
@@ -333,44 +351,82 @@
         for i in range(1, HEAD_DEVS):
             to = lax.rem(x + i, HEAD_DEVS)
             piece = pl.ds(pl.multiple_of(to * BLOCK, BLOCK), BLOCK)
-            gotx.append((chunk, send(
-                part.at[kind, :, piece], recvx.at[kind, i], ssx.at[kind, i], rsx.at[kind, i], (s, to)
-            )))
-        if chunk == 1:
-            for q in range(SEG_DEV):
-                term = weight_end[q] * dot(sin[q], states[q])
-                grad_in[q] = (quad_in[q] + term).astype(BF16)
+            send(part.at[kind, :, piece], recvx.at[kind, i], 8 + chunk, (s, to))
+        return states
+
     own = pl.ds(pl.multiple_of(x * BLOCK, BLOCK), BLOCK)
-    for chunk in range(2):
-        for owner, copy in gotx:
-            if owner == chunk:
-                copy.wait_recv()
+
+    def heads_of(chunk):
         kind = 1 - chunk
+        arrive(8 + chunk, recvx.at[kind, pl.ds(1, HEAD_DEVS - 1)])
         total = part[kind, :, own]
         for i in range(1, HEAD_DEVS):
             total = total + recvx[kind, i]
-        result = grad_sin if kind == 0 else grad_sout
-        result[...] = total
-    for copy in copies:
+        near, far = ((out_sin, grad_sin), (out_sout, grad_sout))[kind]
+        near[...] = total
+        return pltpu.make_async_copy(near, far, osem.at[kind])
+
+    second(0)
+    third(0)
+    second(1)
+    fourth(0)
+    third(1)
+    states_of(0)
+    fourth(1)
+    adjoints = states_of(1)
+    for q in range(SEG_DEV):
+        term = weight_end[q] * dot(sin[q], adjoints[q])
+        out_in[q] = (quad_in[q] + term).astype(BF16)
+    stores = [pltpu.make_async_copy(out_in, grad_in, osem.at[2])]
+    stores[0].start()
+    for chunk in range(2):
+        stores.append(heads_of(chunk))
+        stores[-1].start()
+    for store in stores:
+        store.wait()
+    for copy in pending:
         copy.wait_send()
 
 
+def hand_over(a_in, b_in, c_in, a_out, b_out, c_out, a, b, c, isem, osem):
+    pairs = ((a_in, a), (b_in, b), (c_in, c))
+    loads = [pltpu.make_async_copy(far, near, isem.at[n]) for n, (far, near) in enumerate(pairs)]
+    pairs = ((a, a_out), (b, b_out), (c, c_out))
+    stores = [pltpu.make_async_copy(near, far, osem.at[n]) for n, (near, far) in enumerate(pairs)]
+    for load in loads:
+        load.start()
+    for load, store in zip(loads, stores):
+        load.wait()
+        store.start()
+    for store in stores:
+        store.wait()
+
+
 def shards(inputs, cotangent, state_in, state_out, log_decay, parents, slot_segment):
-    vmem = pl.BlockSpec(memory_space=pltpu.VMEM)
-    smem = pl.BlockSpec(memory_space=pltpu.SMEM)
+    hbm = pl.BlockSpec(memory_space=pltpu.HBM)
     both = SEG_DEV * HEADS_DEV
     slots2 = RING * CORES
     dma = pltpu.SemaphoreType.DMA
-    return pl.pallas_call(
+    grad_state = (SEG_DEV, BLOCK, STATE)
+    shapes = (
+        jax.ShapeDtypeStruct(inputs.shape, BF16),
+        jax.ShapeDtypeStruct(grad_state, F32),
+        jax.ShapeDtypeStruct(grad_state, F32),
+    )
+    results = pl.pallas_call(
         kernel,
-        out_shape=(
-            jax.ShapeDtypeStruct(inputs.shape, BF16),
-            jax.ShapeDtypeStruct((SEG_DEV, BLOCK, STATE), F32),
-            jax.ShapeDtypeStruct((SEG_DEV, BLOCK, STATE), F32),
-        ),
-        in_specs=[vmem] * 5 + [smem] * 2,
-        out_specs=(vmem, vmem, vmem),
+        out_shape=shapes,
+        in_specs=[hbm] * 7,
+        out_specs=(hbm,) * 3,
         scratch_shapes=[
+            pltpu.VMEM(inputs.shape, BF16),
+            pltpu.VMEM(inputs.shape, BF16),
+            pltpu.VMEM(state_in.shape, BF16),
+            pltpu.VMEM(state_in.shape, BF16),
+            pltpu.VMEM(log_decay.shape, F32),
+            pltpu.SMEM(parents.shape, jnp.int32),
+            pltpu.SMEM(parents.shape, jnp.int32),
+            dma((7,)),
             pltpu.VMEM((both, LENGTH), F32),
             pltpu.VMEM((LENGTH, 4 * both), F32),
             pltpu.VMEM((SEG_DEV, LENGTH, WIDTH), F32),
@@ -378,10 +434,10 @@
             pltpu.VMEM((SEG_DEV, LENGTH, WIDTH), BF16),
             pltpu.VMEM((SEG_DEV, LENGTH, WIDTH), F32),
             pltpu.VMEM((2, SEG_DEV, LENGTH, STATE), F32),
-            pltpu.VMEM((2, RING, SEG_DEV * (SLICE + 8), BLOCK), F32),
-            pltpu.VMEM((2, RING, SEG_DEV * (SLICE + 8), BLOCK), F32),
-            pltpu.VMEM((2, RING, SEG_DEV * SLICE, BLOCK), F32),
-            pltpu.VMEM((2, RING, SEG_DEV * SLICE, BLOCK), F32),
+            pltpu.VMEM((2, RING, ROW1 + 8, BLOCK), F32),
+            pltpu.VMEM((2, RING, ROW1 + 8, BLOCK), F32),
+            pltpu.VMEM((2, RING, ROW1, BLOCK), F32),
+            pltpu.VMEM((2, RING, ROW1, BLOCK), F32),
             pltpu.VMEM((2, SLICE, 2 * TABLE, BLOCK), F32),
             pltpu.VMEM((2, slots2, 2 * TABLE, BLOCK), F32),
             pltpu.VMEM((2, SLICE, TABLE, BLOCK), F32),
@@ -392,16 +448,23 @@
             pltpu.VMEM((2, 2, RING, SEG_DEV, SLICE, BLOCK), F32),
             pltpu.VMEM((2, 2, RING, SEG_DEV, SLICE, BLOCK), F32),
             pltpu.VMEM((2, HEAD_DEVS, SEG_DEV, BLOCK, STATE), F32),
-            dma((2, 2, RING)), dma((2, 2, RING)),
-            dma((2, 2, slots2)), dma((2, 2, slots2)),
-            dma((2, 2, slots2)), dma((2, 2, slots2)),
-            dma((2, 2, RING)), dma((2, 2, RING)),
-            dma((2, HEAD_DEVS)), dma((2, HEAD_DEVS)),
+            pltpu.VMEM(inputs.shape, BF16),
+            pltpu.VMEM(grad_state, F32),
+            pltpu.VMEM(grad_state, F32),
+            dma((10,)), dma((10,)), dma((3,)),
         ],
         compiler_params=pltpu.CompilerParams(
-            collective_id=0, has_side_effects=True, vmem_limit_bytes=40 * 2**20
+            collective_id=0, has_side_effects=True, vmem_limit_bytes=60 * 2**20
         ),
     )(inputs, cotangent, state_in, state_out, log_decay, parents, slot_segment)
+    return pl.pallas_call(
+        hand_over,
+        out_shape=shapes,
+        in_specs=[hbm] * 3,
+        out_specs=(hbm,) * 3,
+        scratch_shapes=[pltpu.VMEM(r.shape, r.dtype) for r in results] + [dma((3,)), dma((3,))],
+        compiler_params=pltpu.CompilerParams(vmem_limit_bytes=60 * 2**20),
+    )(*results)
 
 
 def solution(mesh):

time: 68.5 us -> 60.5 us (0.88)
  local copies, waits for them, and re-layouts: 8.15 us -> 0 us
    unnamed x17 -> x0, local copies, waits for them, and re-layouts: 8.15 us -> none
    pallas_call x1 -> x2, Pallas kernels: 59.2 us -> 59.7 us  [the longest x1 57.7 us: shards(): pl.pallas_call(kernel, out_shape=shapes, in_specs=[hbm] * 7, out_specs=(h...]
where the time goes in v2:
time: 60.5 us; the launch traced here: 60.3 us
  Pallas kernels  59.7 us (99%)
  between operations  0.64 us (1%)
    pallas_call x1, Pallas kernels, shards(): pl.pallas_call(kernel, out_shape=shapes, in_specs=[hbm] * 7, out_specs=(h...  57.7 us
    pallas_call x1, Pallas kernels, shards(): pl.pallas_call(hand_over, out_shape=shapes, in_specs=[hbm] * 3, out_specs...  1.96 us

profile of v2, /device:TPU:1, one launch (start us, length us, event | category | flops | bytes accessed | tf_op | source)
XLA Modules:
  0.0 60.3 jit_solution(6279399315592474822)
XLA Ops:
  0.6 57.7 %shard_map.94 = (bf16[2,512,256]{2,1,0:T(8,128)(2,1)}, f32[2,128,128]{2,1,0:T(8,128)}, f32[2,128,128]{2,1,0:T(8,128)}) custom-call(bf16[2,512,256]{2,1,0:T(8,128)(2,1)} %inputs_hbm.1, bf16[2,512,256]{2,1,0:T(8,128)(2,1)} %cotan_hbm.1, bf16[2,512,128]{2,1,0:T(8,128)(2,1)} %sin_hbm.1, bf16[2,512,128]{2,1,0:T(8,128)(2,1)} %sout_hbm.1, f32[2,4,512]{2,1,0:T(4,128)} %ldec_hbm.1, ...), custom_call_target="tpu_custom_call" | custom-call | tf_op jit(solution)/shard_map/pallas_call | solution.py:416
  58.4 2.0 %shard_map.95 = (bf16[2,512,256]{2,1,0:T(8,128)(2,1)}, f32[2,128,128]{2,1,0:T(8,128)}, f32[2,128,128]{2,1,0:T(8,128)}) custom-call(bf16[2,512,256]{2,1,0:T(8,128)(2,1)} %get-tuple-element.6.a_in, f32[2,128,128]{2,1,0:T(8,128)} %get-tuple-element.7.b_in, f32[2,128,128]{2,1,0:T(8,128)} %get-tuple-element.8.c_in), custom_call_target="tpu_custom_call" | custom-call | tf_op jit(solution)/shard_map/pallas_call | solution.py:460

commit v3 on v2

--- a/solution.py
+++ b/solution.py
@@ -12,6 +12,7 @@
 ROOTS = 2
 TABLE = 8
 RING = 8
+ORDER = (4, 3, 5, 2, 6, 1, 7, 0)
 CORES = 2
 HEAD_DEVS = 4
 SEG_DEV = 2
@@ -22,6 +23,7 @@
 STATE = 128
 SLICE = STATE // RING
 BLOCK = 128
+ADJ_AFTER = 1
 ROW1 = SEG_DEV * SLICE
 
 
@@ -179,17 +181,19 @@
 
     rows1 = (pl.ds(0, ROW1 + 1), pl.ds(0, ROW1))
     out1, in1 = (send1f, send1j), (recv1f, recv1j)
-    for chunk in range(2):
-        for i in range(1, RING):
+
+    def first(chunk):
+        for i in ORDER[:-1]:
             for half in range(2):
                 to = lax.rem(mine[half] + i, RING)
                 send(
                     out1[chunk].at[half, to, rows1[chunk]], in1[chunk].at[half, i, rows1[chunk]],
                     chunk, (first_peer(half, i), x),
                 )
-    for half in range(2):
-        recv1f[half, 0, rows1[0]] = send1f[half, mine[half], rows1[0]]
-        recv1j[half, 0] = send1j[half, mine[half]]
+        for half in range(2):
+            in1[chunk][half, 0, rows1[chunk]] = out1[chunk][half, mine[half], rows1[chunk]]
+
+    first(0)
 
     lane = lax.broadcasted_iota(jnp.int32, (BLOCK, BLOCK), 1)
     first_head = lane < HEAD_DIM
@@ -222,6 +226,8 @@
                     term = mask * dot_nt(in_head, cot_pair)
                     coupled = term if coupled is None else coupled + term
                 quad_in[q, here, lanes] = jnp.where(first_head, results[0], results[1])
+            if q == 0 and b == ADJ_AFTER:
+                first(1)
             coupled = coupled.astype(BF16)
             part[0, q, here] = dot(coupled, sout_b)
             read = dot_tn(coupled, sin_b)
@@ -259,9 +265,8 @@
                 out[half, :, pl.ds(TABLE, 1), :] = jnp.broadcast_to(
                     row.reshape(1, 1, BLOCK), (SLICE, 1, BLOCK)
                 )
-        for i in range(RING):
-            for k in range(CORES):
-                for half in range(2):
+            for i in ORDER:
+                for k in range(CORES):
                     to = lax.rem(other[half] + i, RING) * CORES + lax.rem(c + k, CORES)
                     slot = i * CORES + k
                     if slot == 0:
@@ -298,10 +303,9 @@
                 for m in range(ROOTS, TABLE):
                     carried = carried + jnp.where(rank_row == parents[m], product[m : m + 1], 0.0)
                 send3[chunk, half] = total + jnp.where(rank_row < ROOTS, carried, 0.0)
-        for i in range(RING):
-            for k in range(CORES):
-                for half in range(2):
-                    row = other[half] * CORES + c
+            row = other[half] * CORES + c
+            for i in ORDER:
+                for k in range(CORES):
                     if i + k == 0:
                         recv3[chunk, half, row] = send3[chunk, half]
                         continue
@@ -315,8 +319,9 @@
         for half in range(2):
             for k in range(TABLE):
                 table[chunk, half, k] = recv3[chunk, half, :, k, :]
-            for i in range(RING):
-                for q in range(SEG_DEV):
+        for q in range(SEG_DEV):
+            for i in ORDER:
+                for half in range(2):
                     segment = slots[first_peer(half, i) * SEG_DEV + q]
                     if chunk == 0:
                         index = parents[segment]
@@ -325,63 +330,63 @@
                     else:
                         exists = segment < TABLE
                         index = jnp.minimum(segment, TABLE - 1)
-                    picked = table[chunk, half, index]
-                    send4[chunk, half, i, q] = jnp.where(exists, picked, 0.0)
-        for i in range(RING):
-            for half in range(2):
-                row = mine[half]
-                if i == 0:
-                    recv4[chunk, half, row] = send4[chunk, half, 0]
-                    continue
-                send(
-                    send4.at[chunk, half, i], recv4.at[chunk, half, row],
-                    6 + chunk, (first_peer(half, i), x),
-                )
+                    picked = jnp.where(exists, table[chunk, half, index], 0.0)
+                    row = mine[half]
+                    if i == 0:
+                        recv4[chunk, q, half, row] = picked
+                        continue
+                    send4[chunk, q, half, i] = picked
+                    send(
+                        send4.at[chunk, q, half, i], recv4.at[chunk, q, half, row],
+                        6 + 2 * chunk + q, (first_peer(half, i), x),
+                    )
 
     def states_of(chunk):
-        arrive(6 + chunk, recv4.at[chunk, :, pl.ds(0, RING - 1)])
         kind = 1 - chunk
         states = []
         for q in range(SEG_DEV):
-            halves = [recv4[chunk, half, :, q].reshape(STATE, BLOCK) for half in range(2)]
+            arrive(6 + 2 * chunk + q, recv4.at[chunk, q, :, pl.ds(0, RING - 1)])
+            halves = [recv4[chunk, q, half].reshape(STATE, BLOCK) for half in range(2)]
             state = jnp.concatenate(halves, axis=1).astype(BF16)
             states.append(state)
             data = scaled_cot[q] if chunk == 0 else scaled_in[q]
             part[kind, q] = part[kind, q] + dot_nt(data, state)
-        for i in range(1, HEAD_DEVS):
-            to = lax.rem(x + i, HEAD_DEVS)
-            piece = pl.ds(pl.multiple_of(to * BLOCK, BLOCK), BLOCK)
-            send(part.at[kind, :, piece], recvx.at[kind, i], 8 + chunk, (s, to))
+            for i in (2, 1, 3):
+                to = lax.rem(x + i, HEAD_DEVS)
+                piece = pl.ds(pl.multiple_of(to * BLOCK, BLOCK), BLOCK)
+                send(part.at[kind, q, piece], recvx.at[kind, q, i], 10 + 2 * chunk + q, (s, to))
         return states
 
     own = pl.ds(pl.multiple_of(x * BLOCK, BLOCK), BLOCK)
 
     def heads_of(chunk):
         kind = 1 - chunk
-        arrive(8 + chunk, recvx.at[kind, pl.ds(1, HEAD_DEVS - 1)])
-        total = part[kind, :, own]
-        for i in range(1, HEAD_DEVS):
-            total = total + recvx[kind, i]
         near, far = ((out_sin, grad_sin), (out_sout, grad_sout))[kind]
-        near[...] = total
-        return pltpu.make_async_copy(near, far, osem.at[kind])
+        for q in range(SEG_DEV):
+            arrive(10 + 2 * chunk + q, recvx.at[kind, q, pl.ds(1, HEAD_DEVS - 1)])
+            total = part[kind, q, own]
+            for i in range(1, HEAD_DEVS):
+                total = total + recvx[kind, q, i]
+            near[q] = total
+            store = pltpu.make_async_copy(near.at[q], far.at[q], osem.at[2 * kind + q])
+            store.start()
+            stores.append(store)
 
     second(0)
+    second(1)
     third(0)
-    second(1)
+    third(1)
     fourth(0)
-    third(1)
+    fourth(1)
     states_of(0)
-    fourth(1)
     adjoints = states_of(1)
     for q in range(SEG_DEV):
         term = weight_end[q] * dot(sin[q], adjoints[q])
         out_in[q] = (quad_in[q] + term).astype(BF16)
-    stores = [pltpu.make_async_copy(out_in, grad_in, osem.at[2])]
+    stores = [pltpu.make_async_copy(out_in, grad_in, osem.at[4])]
     stores[0].start()
     for chunk in range(2):
-        stores.append(heads_of(chunk))
-        stores[-1].start()
+        heads_of(chunk)
     for store in stores:
         store.wait()
     for copy in pending:
@@ -445,13 +450,13 @@
             pltpu.VMEM((2, 2, TABLE, BLOCK), F32),
             pltpu.VMEM((2, 2, SLICE, TABLE, BLOCK), F32),
             pltpu.VMEM((2, 2, TABLE, SLICE, BLOCK), F32),
-            pltpu.VMEM((2, 2, RING, SEG_DEV, SLICE, BLOCK), F32),
-            pltpu.VMEM((2, 2, RING, SEG_DEV, SLICE, BLOCK), F32),
-            pltpu.VMEM((2, HEAD_DEVS, SEG_DEV, BLOCK, STATE), F32),
+            pltpu.VMEM((2, SEG_DEV, 2, RING, SLICE, BLOCK), F32),
+            pltpu.VMEM((2, SEG_DEV, 2, RING, SLICE, BLOCK), F32),
+            pltpu.VMEM((2, SEG_DEV, HEAD_DEVS, BLOCK, STATE), F32),
             pltpu.VMEM(inputs.shape, BF16),
             pltpu.VMEM(grad_state, F32),
             pltpu.VMEM(grad_state, F32),
-            dma((10,)), dma((10,)), dma((3,)),
+            dma((14,)), dma((14,)), dma((5,)),
         ],
         compiler_params=pltpu.CompilerParams(
             collective_id=0, has_side_effects=True, vmem_limit_bytes=60 * 2**20

time: 60.5 us -> 52.1 us (0.86)
  Pallas kernels: 59.7 us -> 51.2 us
    pallas_call x1, Pallas kernels: 57.7 us -> 49.3 us  [shards(): pl.pallas_call(kernel, out_shape=shapes, in_specs=[hbm] * 7, out_specs=(h...]
where the time goes in v3:
time: 52.1 us; the launch traced here: 51.9 us
  Pallas kernels  51.2 us (98%)
  between operations  0.64 us (1%)
    pallas_call x1, Pallas kernels, shards(): pl.pallas_call(kernel, out_shape=shapes, in_specs=[hbm] * 7, out_specs=(h...  49.3 us
    pallas_call x1, Pallas kernels, shards(): pl.pallas_call(hand_over, out_shape=shapes, in_specs=[hbm] * 3, out_specs...  1.96 us

profile of v3, /device:TPU:1, one launch (start us, length us, event | category | flops | bytes accessed | tf_op | source)
XLA Modules:
  0.0 51.9 jit_solution(9292716365972362956)
XLA Ops:
  0.6 49.3 %shard_map.94 = (bf16[2,512,256]{2,1,0:T(8,128)(2,1)}, f32[2,128,128]{2,1,0:T(8,128)}, f32[2,128,128]{2,1,0:T(8,128)}) custom-call(bf16[2,512,256]{2,1,0:T(8,128)(2,1)} %inputs_hbm.1, bf16[2,512,256]{2,1,0:T(8,128)(2,1)} %cotan_hbm.1, bf16[2,512,128]{2,1,0:T(8,128)(2,1)} %sin_hbm.1, bf16[2,512,128]{2,1,0:T(8,128)(2,1)} %sout_hbm.1, f32[2,4,512]{2,1,0:T(4,128)} %ldec_hbm.1, ...), custom_call_target="tpu_custom_call" | custom-call | tf_op jit(solution)/shard_map/pallas_call | solution.py:421
  49.9 2.0 %shard_map.95 = (bf16[2,512,256]{2,1,0:T(8,128)(2,1)}, f32[2,128,128]{2,1,0:T(8,128)}, f32[2,128,128]{2,1,0:T(8,128)}) custom-call(bf16[2,512,256]{2,1,0:T(8,128)(2,1)} %get-tuple-element.6.a_in, f32[2,128,128]{2,1,0:T(8,128)} %get-tuple-element.7.b_in, f32[2,128,128]{2,1,0:T(8,128)} %get-tuple-element.8.c_in), custom_call_target="tpu_custom_call" | custom-call | tf_op jit(solution)/shard_map/pallas_call | solution.py:465

commit v4 on v3

--- a/solution.py
+++ b/solution.py
@@ -84,18 +84,19 @@
 
     loads = []
     operands = (
-        (ldec_hbm, ldec), (inputs_hbm, inputs), (cotan_hbm, cotan), (sin_hbm, sin),
-        (sout_hbm, sout), (slots_hbm, slots), (parents_hbm, parents),
+        (ldec_hbm, ldec), (inputs_hbm, inputs), (sin_hbm, sin), (slots_hbm, slots),
+        (cotan_hbm, cotan), (sout_hbm, sout), (parents_hbm, parents),
     )
     for n, (far, near) in enumerate(operands):
         load = pltpu.make_async_copy(far, near, lsem.at[n])
+        loads.append(load)
+    for load in loads[:4]:
         load.start()
-        loads.append(load)
 
     barrier = pltpu.get_barrier_semaphore()
     peers = []
-    for half in range(2):
-        for i in range(1, RING):
+    for i in ORDER[:-1]:
+        for half in range(2):
             for k in range(CORES):
                 peers.append((second_peer(half, i, k), x))
     peers.append((seg_index(y, z, lax.rem(c + 1, CORES)), x))
@@ -103,6 +104,8 @@
         peers.append((s, lax.rem(x + i, HEAD_DEVS)))
     for peer in peers:
         pl.semaphore_signal(barrier, inc=1, device_id=peer, device_id_type=MESH)
+    for load in loads[4:]:
+        load.start()
 
     pending = []
 
@@ -147,24 +150,23 @@
     columns = jnp.transpose(columns)
     cum_col[...] = columns
     upper, lower = split(columns)
-    for load in loads[1:]:
+    for load in loads[1:4]:
         load.wait()
     key_row = lax.broadcasted_iota(jnp.int32, (4 * rows, 2 * WIDTH), 0)
     key_lane = lax.broadcasted_iota(jnp.int32, (4 * rows, 2 * WIDTH), 1)
     lane64 = lax.rem(lax.broadcasted_iota(jnp.int32, (1, WIDTH), 1), HEAD_DIM)
     packed = None
+    starts = []
     for q in range(SEG_DEV):
         wanted = (key_lane // WIDTH) * rows + q * HEADS_DEV + lax.rem(key_lane, WIDTH) // HEAD_DIM
         pick = jnp.where(key_row == wanted, 1.0, 0.0).astype(BF16)
         spread = dot(upper, pick) + dot(lower, pick)
         to_end, from_start = spread[:, :WIDTH], spread[:, WIDTH:]
         weight_end[q] = to_end
+        starts.append(from_start)
         s_in = (inputs[q].astype(F32) * to_end).astype(BF16)
-        s_cot = (cotan[q].astype(F32) * from_start).astype(BF16)
         scaled_in[q] = s_in
-        scaled_cot[q] = s_cot
         local_end = dot_tn(sin[q], s_in)
-        local_adj = dot_tn(sout[q], s_cot)
         segment = slots[s * SEG_DEV + q]
         end_decay = jnp.where(lane64 == segment, from_start[LENGTH - 1 : LENGTH], 0.0)
         packed = end_decay if q == 0 else packed + end_decay
@@ -172,7 +174,6 @@
             lanes = slice(half * BLOCK, (half + 1) * BLOCK)
             place = pl.ds(q * SLICE, SLICE)
             send1f[half, :, place, :] = local_end[:, lanes].reshape(RING, SLICE, BLOCK)
-            send1j[half, :, place, :] = local_adj[:, lanes].reshape(RING, SLICE, BLOCK)
     for half in range(2):
         row = packed[:, half * BLOCK : (half + 1) * BLOCK].reshape(1, 1, BLOCK)
         send1f[half, :, pl.ds(ROW1, 1), :] = jnp.broadcast_to(row, (RING, 1, BLOCK))
@@ -194,6 +195,17 @@
             in1[chunk][half, 0, rows1[chunk]] = out1[chunk][half, mine[half], rows1[chunk]]
 
     first(0)
+
+    for load in loads[4:]:
+        load.wait()
+    for q in range(SEG_DEV):
+        s_cot = (cotan[q].astype(F32) * starts[q]).astype(BF16)
+        scaled_cot[q] = s_cot
+        local_adj = dot_tn(sout[q], s_cot)
+        for half in range(2):
+            lanes = slice(half * BLOCK, (half + 1) * BLOCK)
+            place = pl.ds(q * SLICE, SLICE)
+            send1j[half, :, place, :] = local_adj[:, lanes].reshape(RING, SLICE, BLOCK)
 
     lane = lax.broadcasted_iota(jnp.int32, (BLOCK, BLOCK), 1)
     first_head = lane < HEAD_DIM

time: 52.1 us -> 51.7 us (level)
  no operation moved by 1% of the time
where the time goes in v4:
time: 51.7 us; the launch traced here: 51.5 us
  Pallas kernels  50.9 us (98%)
  between operations  0.64 us (1%)
    pallas_call x1, Pallas kernels, shards(): pl.pallas_call(kernel, out_shape=shapes, in_specs=[hbm] * 7, out_specs=(h...  48.9 us
    pallas_call x1, Pallas kernels, shards(): pl.pallas_call(hand_over, out_shape=shapes, in_specs=[hbm] * 3, out_specs...  1.96 us

profile of v4, /device:TPU:1, one launch (start us, length us, event | category | flops | bytes accessed | tf_op | source)
XLA Modules:
  0.0 51.5 jit_solution(2310641521893082167)
XLA Ops:
  0.6 48.9 %shard_map.94 = (bf16[2,512,256]{2,1,0:T(8,128)(2,1)}, f32[2,128,128]{2,1,0:T(8,128)}, f32[2,128,128]{2,1,0:T(8,128)}) custom-call(bf16[2,512,256]{2,1,0:T(8,128)(2,1)} %inputs_hbm.1, bf16[2,512,256]{2,1,0:T(8,128)(2,1)} %cotan_hbm.1, bf16[2,512,128]{2,1,0:T(8,128)(2,1)} %sin_hbm.1, bf16[2,512,128]{2,1,0:T(8,128)(2,1)} %sout_hbm.1, f32[2,4,512]{2,1,0:T(4,128)} %ldec_hbm.1, ...), custom_call_target="tpu_custom_call" | custom-call | tf_op jit(solution)/shard_map/pallas_call | solution.py:433
  49.6 2.0 %shard_map.95 = (bf16[2,512,256]{2,1,0:T(8,128)(2,1)}, f32[2,128,128]{2,1,0:T(8,128)}, f32[2,128,128]{2,1,0:T(8,128)}) custom-call(bf16[2,512,256]{2,1,0:T(8,128)(2,1)} %get-tuple-element.6.a_in, f32[2,128,128]{2,1,0:T(8,128)} %get-tuple-element.7.b_in, f32[2,128,128]{2,1,0:T(8,128)} %get-tuple-element.8.c_in), custom_call_target="tpu_custom_call" | custom-call | tf_op jit(solution)/shard_map/pallas_call | solution.py:477

commit v5 on v4

--- a/solution.py
+++ b/solution.py
@@ -406,10 +406,10 @@
 
 
 def hand_over(a_in, b_in, c_in, a_out, b_out, c_out, a, b, c, isem, osem):
-    pairs = ((a_in, a), (b_in, b), (c_in, c))
-    loads = [pltpu.make_async_copy(far, near, isem.at[n]) for n, (far, near) in enumerate(pairs)]
-    pairs = ((a, a_out), (b, b_out), (c, c_out))
-    stores = [pltpu.make_async_copy(near, far, osem.at[n]) for n, (near, far) in enumerate(pairs)]
+    steps = [(a_in.at[q], a.at[q], a_out.at[q]) for q in range(SEG_DEV)]
+    steps += [(b_in, b, b_out), (c_in, c, c_out)]
+    loads = [pltpu.make_async_copy(u, v, isem.at[n]) for n, (u, v, _) in enumerate(steps)]
+    stores = [pltpu.make_async_copy(v, w, osem.at[n]) for n, (_, v, w) in enumerate(steps)]
     for load in loads:
         load.start()
     for load, store in zip(loads, stores):
@@ -479,7 +479,7 @@
         out_shape=shapes,
         in_specs=[hbm] * 3,
         out_specs=(hbm,) * 3,
-        scratch_shapes=[pltpu.VMEM(r.shape, r.dtype) for r in results] + [dma((3,)), dma((3,))],
+        scratch_shapes=[pltpu.VMEM(r.shape, r.dtype) for r in results] + [dma((4,)), dma((4,))],
         compiler_params=pltpu.CompilerParams(vmem_limit_bytes=60 * 2**20),
     )(*results)
 

time: 51.7 us -> 51.7 us (level)
  no operation moved by 1% of the time
where the time goes in v5:
time: 51.7 us; the launch traced here: 51.5 us
  Pallas kernels  50.8 us (98%)
  between operations  0.64 us (1%)
    pallas_call x1, Pallas kernels, shards(): pl.pallas_call(kernel, out_shape=shapes, in_specs=[hbm] * 7, out_specs=(h...  48.9 us
    pallas_call x1, Pallas kernels, shards(): pl.pallas_call(hand_over, out_shape=shapes, in_specs=[hbm] * 3, out_specs...  1.89 us

profile of v5, /device:TPU:1, one launch (start us, length us, event | category | flops | bytes accessed | tf_op | source)
XLA Modules:
  0.0 51.5 jit_solution(511516070285103858)
XLA Ops:
  0.6 48.9 %shard_map.94 = (bf16[2,512,256]{2,1,0:T(8,128)(2,1)}, f32[2,128,128]{2,1,0:T(8,128)}, f32[2,128,128]{2,1,0:T(8,128)}) custom-call(bf16[2,512,256]{2,1,0:T(8,128)(2,1)} %inputs_hbm.1, bf16[2,512,256]{2,1,0:T(8,128)(2,1)} %cotan_hbm.1, bf16[2,512,128]{2,1,0:T(8,128)(2,1)} %sin_hbm.1, bf16[2,512,128]{2,1,0:T(8,128)(2,1)} %sout_hbm.1, f32[2,4,512]{2,1,0:T(4,128)} %ldec_hbm.1, ...), custom_call_target="tpu_custom_call" | custom-call | tf_op jit(solution)/shard_map/pallas_call | solution.py:433
  49.6 1.9 %shard_map.95 = (bf16[2,512,256]{2,1,0:T(8,128)(2,1)}, f32[2,128,128]{2,1,0:T(8,128)}, f32[2,128,128]{2,1,0:T(8,128)}) custom-call(bf16[2,512,256]{2,1,0:T(8,128)(2,1)} %get-tuple-element.6.a_in, f32[2,128,128]{2,1,0:T(8,128)} %get-tuple-element.7.b_in, f32[2,128,128]{2,1,0:T(8,128)} %get-tuple-element.8.c_in), custom_call_target="tpu_custom_call" | custom-call | tf_op jit(solution)/shard_map/pallas_call | solution.py:477
